TPU v7x, 256 devices: a whole 4x4x8 slice. The times are simulated.
256 devices in a mesh: inner: 16 (over z, core), outer: 16 (over y, x).
Axes of the slice: x: 4, y: 4, z: 8, core: 2. Of those that a mesh axis runs over, the one named last changes fastest.
Arguments:
- acts: bfloat16 [65536, 14848], P(('inner', 'outer')), may hold values from -6 to 6
- key_grad: bfloat16 [65536, 512], P(('inner', 'outer')), may hold values from -0.0234375 to 0.0234375
- shifts: int32 [256, 8], P(('inner', 'outer')), may hold values from 5 to 12, as said below
Outputs:
- weight_grad: float32 [14848, 512], P(('inner', 'outer'))
Inputs may be any that keep to these rules, and one draw needn't show every extreme that they name: `shifts`: column k is the exponent that device uses at hop k; columns from log2(256) on are not used.
All inputs are finite; a program needn't handle non-finite values.
Results may differ from a plain program's by a relative error of at most 0.0053.
Values may be sent and summed in bfloat16 or wider, within the bound.
A program may use at most 128 MiB of HBM per device.

v0:
```python
import jax
import jax.numpy as jnp
from jax import lax
from jax.sharding import PartitionSpec as P

clip_bound = 448.0


def swapped(x, axis, distance):
    return lax.ppermute(x, axis, [(i, i ^ 1 << distance) for i in range(lax.axis_size(axis))])


def power_of_two(shift):
    return jnp.left_shift(jnp.int32(1), shift).astype(jnp.float32)


def quantize(values, shift):
    return jnp.clip(values * power_of_two(shift), -clip_bound, clip_bound).astype(jnp.bfloat16)


def dequantize(packed, shift):
    return packed.astype(jnp.float32) / power_of_two(shift)


def split_rows(partial_value, my_bit):
    half_rows = partial_value.shape[0] // 2
    kept_rows = lax.dynamic_slice_in_dim(partial_value, my_bit * half_rows, half_rows, 0)
    given_rows = lax.dynamic_slice_in_dim(partial_value, (1 - my_bit) * half_rows, half_rows, 0)
    return (kept_rows, given_rows)


def product_over_tokens(left, right):
    return lax.dot_general(
        left, right, (((0,), (0,)), ((), ())), preferred_element_type=jnp.float32
    )


def body(acts, key_grad, shifts):
    inner_size = lax.axis_size("inner")
    outer_size = lax.axis_size("outer")
    inner_bits = inner_size.bit_length() - 1
    outer_bits = outer_size.bit_length() - 1
    inner_at = lax.axis_index("inner")
    outer_at = lax.axis_index("outer")
    mine = inner_at * outer_size + outer_at
    shift_table = lax.all_gather(shifts, ("inner", "outer"), axis=0, tiled=True)
    own_shifts = shifts[0]
    partial_value = product_over_tokens(acts, key_grad)
    start_hop = 0
    for hop_index in range(start_hop, inner_bits):
        bit_pos = inner_bits - 1 - hop_index
        my_bit = jnp.bitwise_and(jnp.right_shift(inner_at, bit_pos), 1)
        kept_rows, given_rows = split_rows(partial_value, my_bit)
        received = swapped(quantize(given_rows, own_shifts[hop_index]), "inner", bit_pos)
        partner = jnp.bitwise_xor(mine, 1 << bit_pos + outer_bits)
        partial_value = kept_rows + dequantize(received, shift_table[partner, hop_index])
    for outer_hop in range(outer_bits):
        hop_index = inner_bits + outer_hop
        bit_pos = outer_bits - 1 - outer_hop
        my_bit = jnp.bitwise_and(jnp.right_shift(outer_at, bit_pos), 1)
        kept_rows, given_rows = split_rows(partial_value, my_bit)
        received = swapped(quantize(given_rows, own_shifts[hop_index]), "outer", bit_pos)
        partner = jnp.bitwise_xor(mine, 1 << bit_pos)
        partial_value = kept_rows + dequantize(received, shift_table[partner, hop_index])
    return partial_value


def solution(mesh):
    return jax.shard_map(
        body,
        mesh=mesh,
        in_specs=(
            P(("inner", "outer"), None),
            P(("inner", "outer"), None),
            P(("inner", "outer"), None),
        ),
        out_specs=P(("inner", "outer"), None),
        check_vma=False,
    )
```

profile of v0, /device:TPU:1, one launch (start us, length us, event | category | flops | bytes accessed | tf_op | source)
XLA Modules:
  0.0 726.1 jit_solution(3086305475823055229)
XLA Ops:
  0.0 1.6 fusion
  2.3 15.3 %fusion.1 = f32[14848,512]{1,0:T(8,128)} fusion(bf16[256,14848]{1,0:T(8,128)(2,1)} %param.3, bf16[256,512]{1,0:T(8,128)(2,1)S(1)} %copy-done), kind=kOutput, calls=%fused_computation.25 | convolution fusion | flops 3892314112 | bytes 38273024 | tf_op jit(solution)/shard_map/dot_general | solution.py:33
  17.6 10.6 %clamp_convert_fusion = bf16[7424,512]{1,0:T(8,128)(2,1)} fusion(f32[14848,512]{1,0:T(8,128)} %fusion.1, s32[]{:T(128)S(6)} %select_n.73, f32[]{:T(128)} %bitcast), kind=kLoop, calls=%fused_computation.1 | loop fusion | flops 11403264 | bytes 22806536 | tf_op jit(solution)/shard_map/convert_element_type | solution.py:18
  28.2 7.7 %collective-permute-start = (bf16[7424,512]{1,0:T(8,128)(2,1)}, bf16[7424,512]{1,0:T(8,128)(2,1)}, u32[]{:S(2)}, u32[]{:S(2)}) collective-permute-start(bf16[7424,512]{1,0:T(8,128)(2,1)} %clamp_convert_fusion), channel_id=1, source_target_pairs={{0,128},{16,144},{32,160},{48,176},{64,192},{80,208},{96,224},{112... | collective-permute-start | bytes 22806536 | tf_op jit(solution)/shard_map/ppermute | solution.py:10
  36.0 410.4 %all-gather = s32[256,1,8]{2,1,0:T(1,128)S(1)} all-gather(s32[1,1,8]{2,1,0:T(1,128)S(1)} %bitcast.19), channel_id=1, replica_groups=mesh['inner'=16,'outer'=16] {'inner','outer'}, dimensions={0}, use_global_device_ids=true | all-gather | bytes 8224 | tf_op jit(solution)/shard_map/all_gather | solution.py:46
  448.4 8.5 %divide_add_fusion = f32[7424,512]{1,0:T(8,128)S(1)} fusion(bf16[7424,512]{1,0:T(8,128)(2,1)} %collective-permute-done, f32[14848,512]{1,0:T(8,128)} %fusion.1, s32[]{:T(128)S(6)} %select_n.72, f32[]{:T(128)} %bitcast.2), kind=kLoop, calls=%fused_computation | loop fusion | flops 11403264 | bytes 38010888 | tf_op jit(solution)/shard_map/add | solution.py:56
  456.9 5.4 copy-done.2
  462.3 2.9 clamp_convert_fusion.1
  466.5 164.6 %collective-permute-done.1 = bf16[3712,512]{1,0:T(8,128)(2,1)} collective-permute-done((bf16[3712,512]{1,0:T(8,128)(2,1)}, bf16[3712,512]{1,0:T(8,128)(2,1)}, u32[]{:S(2)}, u32[]{:S(2)}) %collective-permute-start.1) | collective-permute-done | bytes 3801120 | tf_op jit(solution)/shard_map/ppermute | solution.py:10
  631.2 5.5 divide_add_fusion.1
  636.7 3.0 copy-done.3
  639.7 1.9 clamp_convert_fusion.2
  642.8 41.5 %collective-permute-done.2 = bf16[1856,512]{1,0:T(8,128)(2,1)S(1)} collective-permute-done((bf16[1856,512]{1,0:T(8,128)(2,1)}, bf16[1856,512]{1,0:T(8,128)(2,1)S(1)}, u32[]{:S(2)}, u32[]{:S(2)}) %collective-permute-start.2) | collective-permute-done | bytes 1900576 | tf_op jit(solution)/shard_map/ppermute | solution.py:10
  684.3 2.7 divide_add_fusion.2
  687.1 1.8 copy-done.4
  689.1 1.6 collective-permute-start.3
  692.9 1.8 divide_add_fusion.3
  696.9 11.7 %collective-permute-done.4 = bf16[464,512]{1,0:T(8,128)(2,1)S(1)} collective-permute-done((bf16[464,512]{1,0:T(8,128)(2,1)S(1)}, bf16[464,512]{1,0:T(8,128)(2,1)S(1)}, u32[]{:S(2)}, u32[]{:S(2)}) %collective-permute-start.4) | collective-permute-done | bytes 475168 | tf_op jit(solution)/shard_map/ppermute | solution.py:10
  709.3 1.2 divide_add_fusion.4
  710.5 1.1 collective-permute-start.5
  712.9 3.8 collective-permute-done.5
  716.8 2.7 collective-permute-start.6
  720.9 1.2 collective-permute-done.6
  723.8 1.6 collective-permute-done.7
  (26 shorter events, 5.4 us)
Async XLA Ops:
  0.0 2.3 copy-start
  17.6 18.4 %copy-start.6 = (s32[1,8]{1,0:T(1,128)S(1)}, s32[1,8]{1,0:T(1,128)}, u32[]{:S(2)}) copy-start(s32[1,8]{1,0:T(1,128)} %param.5) | copy-start | bytes 100
  28.2 420.2 %collective-permute-start = (bf16[7424,512]{1,0:T(8,128)(2,1)}, bf16[7424,512]{1,0:T(8,128)(2,1)}, u32[]{:S(2)}, u32[]{:S(2)}) collective-permute-start(bf16[7424,512]{1,0:T(8,128)(2,1)} %clamp_convert_fusion), channel_id=1, source_target_pairs={{0,128},{16,144},{32,160},{48,176},{64,192},{80,208},{96,224},{112... | collective-permute-start | bytes 22806536 | tf_op jit(solution)/shard_map/ppermute | solution.py:10
  456.9 5.4 copy-start.2
  465.2 166.0 %collective-permute-start.1 = (bf16[3712,512]{1,0:T(8,128)(2,1)}, bf16[3712,512]{1,0:T(8,128)(2,1)}, u32[]{:S(2)}, u32[]{:S(2)}) collective-permute-start(bf16[3712,512]{1,0:T(8,128)(2,1)} %clamp_convert_fusion.1), channel_id=1, source_target_pairs={{0,64},{16,80},{32,96},{48,112},{64,0},{80,16},{96,32},{112,48},{1... | collective-permute-start | bytes 11403272 | tf_op jit(solution)/shard_map/ppermute | solution.py:10
  636.7 3.0 copy-start.3
  641.6 42.7 %collective-permute-start.2 = (bf16[1856,512]{1,0:T(8,128)(2,1)}, bf16[1856,512]{1,0:T(8,128)(2,1)S(1)}, u32[]{:S(2)}, u32[]{:S(2)}) collective-permute-start(bf16[1856,512]{1,0:T(8,128)(2,1)} %clamp_convert_fusion.2), channel_id=1, source_target_pairs={{0,32},{16,48},{32,0},{48,16},{64,96},{80,112},{96,64},{112,80},{1... | collective-permute-start | bytes 5701640 | tf_op jit(solution)/shard_map/ppermute | solution.py:10
  684.3 41.8 %copy-start.1 = (bf16[256,512]{1,0:T(8,128)(2,1)S(1)}, bf16[256,512]{1,0:T(8,128)(2,1)}, u32[]{:S(2)}) copy-start(bf16[256,512]{1,0:T(8,128)(2,1)} %param.4) | copy-start | bytes 786436
  687.1 1.8 copy-start.4
  689.1 3.8 collective-permute-start.3
  694.8 13.7 %collective-permute-start.4 = (bf16[464,512]{1,0:T(8,128)(2,1)S(1)}, bf16[464,512]{1,0:T(8,128)(2,1)S(1)}, u32[]{:S(2)}, u32[]{:S(2)}) collective-permute-start(bf16[464,512]{1,0:T(8,128)(2,1)S(1)} %clamp_convert_fusion.4), channel_id=1, source_target_pairs={{0,8},{1,9},{2,10},{3,11},{4,12},{5,13},{6,14},{7,15},{8,0},{9,1},... | collective-permute-start | bytes 1425416 | tf_op jit(solution)/shard_map/ppermute | solution.py:10
  708.5 0.8 copy-start.5
  710.5 6.2 collective-permute-start.5
  716.8 5.3 collective-permute-start.6
  722.2 3.2 collective-permute-start.7
where the time goes:
time: 730 us; the launch traced here: 726 us
  blocking collectives  410 us (56%)
  waiting for transfers between devices  225 us (31%)
  other arithmetic  36.5 us (5%)
  matrix products  15.3 us (2%)
  starting transfers between devices  14.9 us (2%)
  local copies, waits for them, and re-layouts  13.3 us (2%)
  between operations  10.3 us (1%)
    all_gather x1, blocking collectives, body(): shift_table = lax.all_gather(shifts, ('inner', 'outer'), axis=0, tiled=True)  410 us
    ppermute x8, waiting for transfers between devices, swapped(): lax.ppermute(x, axis, [(i, i ^ 1 << distance) for i in range(lax.axis_siz...  225 us
    add x8, other arithmetic, body(): kept_rows + dequantize(received, shift_table[partner, hop_index])  20.5 us
    convert_element_type x8, other arithmetic, quantize(): jnp.clip(values * power_of_two(shift), -clip_bound, clip_bound)  16 us
    dot_general x1, matrix products, product_over_tokens(): lax.dot_general(left, right, (((0,), (0,)), ((), ())), preferred_element_...  15.3 us
    ppermute x8, starting transfers between devices, swapped(): lax.ppermute(x, axis, [(i, i ^ 1 << distance) for i in range(lax.axis_siz...  14.9 us
  transfers between devices with their start and end apart: 8, of which 7 were waited for; matrix products, arithmetic and copies ran while one was open for 0% of the time, Pallas kernels for 0%

commit v1 on v0

v1 whole, which is shorter than its diff:
```python
import functools

import jax
import jax.numpy as jnp
from jax import lax
from jax.experimental import pallas as pl
from jax.experimental.pallas import tpu as pltpu
from jax.sharding import PartitionSpec as P

MESH = pl.DeviceIdType.MESH
BOUND_ROWS = 16


def xor(a, b, bits):
    total = 0
    for bit in range(bits):
        step = 1 << bit
        total = total + step * lax.rem(lax.div(a, step) + lax.div(b, step), 2)
    return total


def clipped(values, bound):
    return jnp.clip(values, -bound, bound).astype(jnp.bfloat16).astype(jnp.float32)


def aligned(index):
    return pl.multiple_of(index, 16)


def round_up(value, unit):
    return -(-value // unit) * unit


def kernel(
    ni,
    no,
    parts,
    span,
    acts_hbm,
    grad_hbm,
    shifts_smem,
    out_ref,
    raw,
    acts_t,
    recv,
    relay,
    grads,
    sums,
    total,
    place,
    place_last,
    out_box,
    in_box,
    limit_box,
    limits_in,
    fetch_sem,
    grad_sem,
    ring_send,
    ring_recv,
    twin_send,
    twin_recv,
    block_send,
    block_recv,
    hop1_send,
    hop1_recv,
    hop2_send,
    hop2_recv,
    local_sem,
    out_send,
    out_recv,
    limit_send,
    limit_recv,
):
    tokens, width = raw.shape
    keys = grads.shape[2]
    block = width // ni
    rows = block // no
    nz = ni // 2
    half = nz // 2
    first = half // 2
    ibits = ni.bit_length() - 1
    obits = no.bit_length() - 1
    quarters = 4
    strip = width // quarters
    count = len(parts)

    i_at = lax.axis_index("inner")
    o_at = lax.axis_index("outer")
    z_at = lax.div(i_at, 2)
    core = lax.rem(i_at, 2)

    def z_off(step):
        return lax.rem(z_at + step + nz, nz)

    def at_inner(z, k):
        return (2 * z + k, o_at)

    def fetch(q):
        cols = pl.ds(q * strip, strip)
        return pltpu.make_async_copy(acts_hbm.at[:, cols], raw.at[:, cols], fetch_sem.at[q])

    grad_copy = pltpu.make_async_copy(grad_hbm, grads.at[i_at, pl.ds(0, tokens)], grad_sem)
    grad_copy.start()
    for q in range(quarters):
        fetch(q).start()

    barrier = pltpu.get_barrier_semaphore()
    for step in range(1, ni):
        pl.semaphore_signal(
            barrier, inc=1, device_id=(lax.rem(i_at + step, ni), o_at), device_id_type=MESH
        )
    for step in range(1, no):
        pl.semaphore_signal(
            barrier, inc=1, device_id=(i_at, lax.rem(o_at + step, no)), device_id_type=MESH
        )

    row_at = lax.broadcasted_iota(jnp.int32, (BOUND_ROWS, keys), 0)
    left_shift = jnp.zeros((BOUND_ROWS, keys), jnp.int32)
    for hop in range(ibits + obits):
        left_shift = jnp.where(row_at == hop, 12 - shifts_smem[0, hop], left_shift)
    own_limits = jnp.left_shift(jnp.ones_like(left_shift), left_shift).astype(jnp.float32) * 0.109375
    own_limits = own_limits.astype(jnp.bfloat16)
    limit_box[...] = own_limits

    def fill_place(ref, piece):
        size = ref.shape[0]
        row = lax.broadcasted_iota(jnp.int32, (size, 128), 0)
        lane = lax.broadcasted_iota(jnp.int32, (size, 128), 1)
        owner = lax.div(row, piece)
        offset = lane - (owner * rows + row - owner * piece)
        for n in range(span // 128):
            ref[:, pl.ds(n * 128, 128)] = offset + n * 128

    fill_place(place, parts[0][3])
    if place_last is not None:
        fill_place(place_last, parts[-1][3])

    grad_copy.wait()
    grads[i_at, pl.ds(tokens, BOUND_ROWS), :] = own_limits

    pl.semaphore_wait(barrier, ni + no - 2)

    grad_rows = grads.shape[1]
    cut = round_up(grad_rows // 2, 16)

    def ring(way, step):
        sign = 1 if way == 0 else -1
        source = 2 * z_off(sign * (1 - step)) + core
        if step < half:
            piece_at = pl.ds(0, grad_rows)
        else:
            piece_at = pl.ds(0, cut) if way == 0 else pl.ds(cut, grad_rows - cut)
        piece = grads.at[source, piece_at]
        return pltpu.make_async_remote_copy(
            src_ref=piece,
            dst_ref=piece,
            send_sem=ring_send.at[way, step - 1],
            recv_sem=ring_recv.at[way, step - 1],
            device_id=at_inner(z_off(sign), core),
            device_id_type=MESH,
        )

    def twin(offset, side):
        source = 2 * z_off(offset) + side
        return pltpu.make_async_remote_copy(
            src_ref=grads.at[source],
            dst_ref=grads.at[source],
            send_sem=twin_send.at[offset % nz],
            recv_sem=twin_recv.at[offset % nz],
            device_id=at_inner(z_at, 1 - core),
            device_id_type=MESH,
        )

    def ring_arrived(step):
        ring(0, step).wait_recv()
        ring(1, step).wait_recv()
        if step < half:
            ring(0, step + 1).start()
            ring(1, step + 1).start()
            twin(-step, core).start()
            twin(step, core).start()
        else:
            twin(half, core).start()

    def limit_copy(target):
        return pltpu.make_async_remote_copy(
            src_ref=limit_box,
            dst_ref=limits_in.at[o_at],
            send_sem=limit_send.at[target],
            recv_sem=limit_recv.at[o_at],
            device_id=(i_at, target),
            device_id_type=MESH,
        )

    def limit_arrival(source):
        return pltpu.make_async_remote_copy(
            src_ref=limit_box,
            dst_ref=limits_in.at[source],
            send_sem=limit_send.at[source],
            recv_sem=limit_recv.at[source],
            device_id=(i_at, source),
            device_id_type=MESH,
        )

    def turn(part, target):
        start, size, at, piece = parts[part]
        column = target * block
        tile = lax.div(column, 128)
        source = place if piece == parts[0][3] else place_last
        pick = (source[...] == column - tile * 128 + at).astype(jnp.bfloat16)
        window = raw[:, pl.ds(pl.multiple_of(tile * 128, 128), span)]
        acts_t[pl.ds(aligned(column + start), size), :] = lax.dot_general(
            pick, window, (((1,), (1,)), ((), ())), preferred_element_type=jnp.float32
        ).astype(jnp.bfloat16)

    def block_copy(part, target):
        start, size = parts[part][:2]
        slot = xor(i_at, target, ibits)
        return pltpu.make_async_remote_copy(
            src_ref=acts_t.at[pl.ds(aligned(target * block + start), size)],
            dst_ref=recv.at[slot, pl.ds(start, size)],
            send_sem=block_send.at[part, slot],
            recv_sem=block_recv.at[part, slot],
            device_id=(target, o_at),
            device_id_type=MESH,
        )

    def halves(part):
        start, size = parts[part][:2]
        low = round_up(size // 2, 16)
        return ((start, low), (start + low, size - low))

    def hop1(part, way, k):
        start, size = halves(part)[way]
        sign = 1 if way == 0 else -1
        target = 2 * z_off(half) + k
        return pltpu.make_async_remote_copy(
            src_ref=acts_t.at[pl.ds(aligned(target * block + start), size)],
            dst_ref=relay.at[k, pl.ds(start, size)],
            send_sem=hop1_send.at[part, way, k],
            recv_sem=hop1_recv.at[part, way, k],
            device_id=at_inner(z_off(sign * first), core),
            device_id_type=MESH,
        )

    def hop2(part, way, k):
        start, size = halves(part)[way]
        sign = 1 if way == 0 else -1
        differ = lax.rem(core + k, 2)
        return pltpu.make_async_remote_copy(
            src_ref=relay.at[k, pl.ds(start, size)],
            dst_ref=recv.at[2 * half + differ, pl.ds(start, size)],
            send_sem=hop2_send.at[part, way, differ],
            recv_sem=hop2_recv.at[part, way, differ],
            device_id=at_inner(z_off(sign * (half - first)), k),
            device_id_type=MESH,
        )

    def hop2_arrival(part, way, differ):
        start, size = halves(part)[way]
        piece = recv.at[2 * half + differ, pl.ds(start, size)]
        return pltpu.make_async_remote_copy(
            src_ref=piece,
            dst_ref=piece,
            send_sem=hop2_send.at[part, way, differ],
            recv_sem=hop2_recv.at[part, way, differ],
            device_id=at_inner(z_off(half), core),
            device_id_type=MESH,
        )

    def block_arrival(part, slot):
        start, size = parts[part][:2]
        piece = recv.at[slot, pl.ds(start, size)]
        return pltpu.make_async_remote_copy(
            src_ref=piece,
            dst_ref=piece,
            send_sem=block_send.at[part, slot],
            recv_sem=block_recv.at[part, slot],
            device_id=at_inner(z_at, 1 - core),
            device_id_type=MESH,
        )

    def local_copy(part):
        start, size = parts[part][:2]
        return pltpu.make_async_copy(
            acts_t.at[pl.ds(aligned(i_at * block + start), size)],
            recv.at[0, pl.ds(start, size)],
            local_sem.at[part],
        )

    def send_steps(part, low, high):
        def one(step, carry):
            odd = lax.rem(step, 2)
            offset = (2 * odd - 1) * (half - lax.div(step + odd, 2))
            z = z_off(offset)
            for k in range(2):
                turn(part, 2 * z + k)

            @pl.when(step == 0)
            def _():
                for way in range(2):
                    for k in range(2):
                        hop1(part, way, k).start()

            @pl.when(jnp.logical_and(step > 0, step < nz - 1))
            def _():
                for k in range(2):
                    block_copy(part, 2 * z + k).start()

            @pl.when(step == nz - 1)
            def _():
                block_copy(part, 2 * z_at + 1 - core).start()
                local_copy(part).start()

            return carry

        lax.fori_loop(low, high, one, 0)

    def forward(part):
        for way in range(2):
            for k in range(2):
                hop1(part, way, k).wait_recv()
                hop2(part, way, k).start()

    ring(0, 1).start()
    ring(1, 1).start()
    twin(0, core).start()
    for step in range(1, no):
        limit_copy(lax.rem(o_at + step, no)).start()
    for q in range(quarters):
        fetch(q).wait()
    done = 0
    for step in range(1, half):
        upto = 2 * step + 1 if step < half - 1 else nz
        send_steps(0, done, upto)
        ring_arrived(step)
        done = upto
    if half == 1:
        send_steps(0, 0, nz)
    send_steps(1, 0, 3)
    ring_arrived(half)
    send_steps(1, 3, nz)
    forward(0)

    def leaf(slot, start, size):
        source = xor(i_at, slot, ibits)
        value = jnp.dot(
            recv[slot, pl.ds(start, size), :],
            grads[source, pl.ds(0, tokens), :],
            preferred_element_type=jnp.float32,
        )
        limit = grads[source, pl.ds(tokens, BOUND_ROWS), :].astype(jnp.float32)
        return value, limit

    def out_copy(part, target):
        piece_at = pl.ds(parts[part][2], 16)
        return pltpu.make_async_remote_copy(
            src_ref=out_box.at[target, piece_at],
            dst_ref=in_box.at[o_at, piece_at],
            send_sem=out_send.at[part, target],
            recv_sem=out_recv.at[part, o_at],
            device_id=(i_at, target),
            device_id_type=MESH,
        )

    def out_arrival(part, source):
        piece_at = pl.ds(parts[part][2], 16)
        return pltpu.make_async_remote_copy(
            src_ref=in_box.at[source, piece_at],
            dst_ref=in_box.at[source, piece_at],
            send_sem=out_send.at[part, source],
            recv_sem=out_recv.at[part, source],
            device_id=(i_at, source),
            device_id_type=MESH,
        )

    quarter = ni // 4

    def work(part):
        start, size, at, piece = parts[part]

        def group(n, carry):
            kept, _ = leaf(n, start, size)
            given, limit = leaf(n + 2 * quarter, start, size)
            first_sum = kept + clipped(given, limit[0:1])
            kept, limit_1 = leaf(n + quarter, start, size)
            given, limit = leaf(n + 3 * quarter, start, size)
            second_sum = kept + clipped(given, limit[0:1])
            sums[n, pl.ds(0, size), :] = first_sum + clipped(second_sum, limit_1[1:2])
            return carry

        lax.fori_loop(0, quarter, group, 0)
        level = 2
        width_now = quarter
        while width_now > 1:
            width_now //= 2
            for n in range(width_now):
                source = xor(i_at, n + width_now, ibits)
                limit = grads[source, pl.ds(tokens, BOUND_ROWS), :].astype(jnp.float32)
                value = sums[n, pl.ds(0, size), :] + clipped(
                    sums[n + width_now, pl.ds(0, size), :], limit[level : level + 1]
                )
                if width_now == 1:
                    total[pl.ds(0, size), :] = value
                else:
                    sums[n, pl.ds(0, size), :] = value
            level += 1
        for owner in range(no):
            out_box[owner, pl.ds(at, 16), :] = total[pl.ds(owner * piece, 16), :].astype(
                jnp.bfloat16
            )
        for step in range(1, no):
            out_copy(part, lax.rem(o_at + step, no)).start()

    def finish(part):
        _, _, at, piece = parts[part]
        for step in range(1, no):
            out_arrival(part, lax.rem(o_at + step, no)).wait_recv()
        leaves = [out_box[o_at, pl.ds(at, 16), :].astype(jnp.float32)]
        limits = [None]
        for slot in range(1, no):
            source = xor(o_at, slot, obits)
            leaves.append(in_box[source, pl.ds(at, 16), :].astype(jnp.float32))
            limits.append(limits_in[source].astype(jnp.float32))
        many = no
        for hop in range(obits):
            many //= 2
            level = ibits + hop
            leaves = [
                leaves[n] + clipped(leaves[n + many], limits[n + many][level : level + 1])
                for n in range(many)
            ]
        out_ref[pl.ds(at, piece), :] = leaves[0][0:piece]

    for part in range(count):
        local_copy(part).wait()
        for slot in range(1, ni):
            if slot // 2 == half:
                for way in range(2):
                    hop2_arrival(part, way, slot % 2).wait_recv()
            else:
                block_arrival(part, slot).wait_recv()
        if part + 1 < count:
            forward(part + 1)
        if part + 2 < count:
            send_steps(part + 2, 0, nz)
        if part == 0:
            for offset in range(nz):
                twin(offset, 1 - core).wait_recv()
            for step in range(1, no):
                limit_arrival(lax.rem(o_at + step, no)).wait_recv()
        work(part)
        if part > 0:
            finish(part - 1)
    finish(count - 1)

    for way in range(2):
        for step in range(1, half + 1):
            ring(way, step).wait_send()
    for offset in range(nz):
        twin(offset, core).wait_send()
    for part in range(count):
        for slot in range(1, ni):
            if slot // 2 != half:
                block_arrival(part, slot).wait_send()
        for way in range(2):
            for k in range(2):
                hop1(part, way, k).wait_send()
                hop2(part, way, k).wait_send()
        for step in range(1, no):
            out_copy(part, lax.rem(o_at + step, no)).wait_send()
    for step in range(1, no):
        limit_copy(lax.rem(o_at + step, no)).wait_send()


def cut_parts(rows, no):
    return tuple(
        (no * at, no * min(16, rows - at), at, min(16, rows - at)) for at in range(0, rows, 16)
    )


def body(acts, key_grad, shifts):
    ni = lax.axis_size("inner")
    no = lax.axis_size("outer")
    tokens, width = acts.shape
    keys = key_grad.shape[1]
    block = width // ni
    rows = block // no
    nz = ni // 2
    half = nz // 2
    parts = cut_parts(rows, no)
    count = len(parts)
    widest = parts[0][1]
    span = max(
        round_up(block * (n + 1), 128) - block * n // 128 * 128 for n in range(ni)
    )
    padded = round_up(rows, 16)
    dma = pltpu.SemaphoreType.DMA
    return pl.pallas_call(
        functools.partial(kernel, ni, no, parts, span),
        out_shape=jax.ShapeDtypeStruct((rows, keys), jnp.float32),
        in_specs=[
            pl.BlockSpec(memory_space=pl.ANY),
            pl.BlockSpec(memory_space=pl.ANY),
            pl.BlockSpec(memory_space=pltpu.SMEM),
        ],
        out_specs=pl.BlockSpec(memory_space=pltpu.VMEM),
        scratch_shapes=[
            pltpu.VMEM((tokens, width), jnp.bfloat16),
            pltpu.VMEM((width, tokens), jnp.bfloat16),
            pltpu.VMEM((ni, block, tokens), jnp.bfloat16),
            pltpu.VMEM((2, block, tokens), jnp.bfloat16),
            pltpu.VMEM((ni, tokens + BOUND_ROWS, keys), jnp.bfloat16),
            pltpu.VMEM((ni // 4, widest, keys), jnp.float32),
            pltpu.VMEM((widest, keys), jnp.float32),
            pltpu.VMEM((widest, span), jnp.int32),
            pltpu.VMEM((parts[-1][1], span), jnp.int32),
            pltpu.VMEM((no, padded, keys), jnp.bfloat16),
            pltpu.VMEM((no, padded, keys), jnp.bfloat16),
            pltpu.VMEM((BOUND_ROWS, keys), jnp.bfloat16),
            pltpu.VMEM((no, BOUND_ROWS, keys), jnp.bfloat16),
            dma((4,)),
            dma,
            dma((2, half)),
            dma((2, half)),
            dma((nz,)),
            dma((nz,)),
            dma((count, ni)),
            dma((count, ni)),
            dma((count, 2, 2)),
            dma((count, 2, 2)),
            dma((count, 2, 2)),
            dma((count, 2, 2)),
            dma((count,)),
            dma((count, no)),
            dma((count, no)),
            dma((no,)),
            dma((no,)),
        ],
        compiler_params=pltpu.CompilerParams(
            collective_id=0, has_side_effects=True, vmem_limit_bytes=56 * 1024 * 1024
        ),
        cost_estimate=pl.CostEstimate(
            flops=2 * tokens * width * keys, bytes_accessed=2 * tokens * width, transcendentals=0
        ),
    )(acts, key_grad, shifts)


def solution(mesh):
    return jax.shard_map(
        body,
        mesh=mesh,
        in_specs=(
            P(("inner", "outer"), None),
            P(("inner", "outer"), None),
            P(("inner", "outer"), None),
        ),
        out_specs=P(("inner", "outer"), None),
        check_vma=False,
    )
```

time: 730 us -> 213 us (0.29)
  blocking collectives: 410 us -> 0 us
  waiting for transfers between devices: 225 us -> 0 us
  Pallas kernels: 0 us -> 211 us
  other arithmetic: 36.5 us -> 0 us
  matrix products: 15.3 us -> 0 us
  starting transfers between devices: 14.9 us -> 0 us
  local copies, waits for them, and re-layouts: 13.3 us -> 1.57 us
  between operations: 10.3 us -> 0.01 us
    all_gather x1 -> x0, blocking collectives: 410 us -> none  [body(): shift_table = lax.all_gather(shifts, ('inner', 'outer'), axis=0, tiled=True)]
    ppermute x8 -> x0, waiting for transfers between devices: 225 us -> none  [swapped(): lax.ppermute(x, axis, [(i, i ^ 1 << distance) for i in range(lax.axis_siz...]
    pallas_call x0 -> x1, Pallas kernels: none -> 211 us  [body(): pl.pallas_call(functools.partial(kernel, ni, no, parts, span), out_shape=...]
    add x8 -> x0, other arithmetic: 20.5 us -> none  [body(): kept_rows + dequantize(received, shift_table[partner, hop_index])]
    convert_element_type x8 -> x0, other arithmetic: 16 us -> none  [quantize(): jnp.clip(values * power_of_two(shift), -clip_bound, clip_bound)]
    dot_general x1 -> x0, matrix products: 15.3 us -> none  [product_over_tokens(): lax.dot_general(left, right, (((0,), (0,)), ((), ())), preferred_element_...]
    ppermute x8 -> x0, starting transfers between devices: 14.9 us -> none  [swapped(): lax.ppermute(x, axis, [(i, i ^ 1 << distance) for i in range(lax.axis_siz...]
    unnamed x14 -> x1, local copies, waits for them, and re-layouts: 11 us -> 1.57 us
  transfers between devices with their start and end apart: 8 -> 0, of which waited for: 7 -> 0; matrix products, arithmetic and copies ran while one was open for 0% -> 0% of each run, Pallas kernels for 0% -> 0%
where the time goes in v1:
time: 213 us; the launch traced here: 212 us
  Pallas kernels  211 us (99%)
    pallas_call x1, Pallas kernels, body(): pl.pallas_call(functools.partial(kernel, ni, no, parts, span), out_shape=...  211 us

profile of v1, /device:TPU:1, one launch (start us, length us, event | category | flops | bytes accessed | tf_op | source)
XLA Modules:
  0.0 212.4 jit_solution(17605159687138978865)
XLA Ops:
  0.0 210.9 %shard_map.37 = f32[58,512]{1,0:T(8,128)} custom-call(bf16[256,14848]{1,0:T(8,128)(2,1)} %acts_hbm.1, bf16[256,512]{1,0:T(8,128)(2,1)} %grad_hbm.1, s32[1,8]{1,0:T(1,128)} %shifts_smem.1), custom_call_target="tpu_custom_call" | custom-call | flops 3892314112 | bytes 7602176 | tf_op jit(solution)/shard_map/pallas_call | solution.py:499
  210.9 1.6 copy.5

commit v2 on v1

--- a/solution.py
+++ b/solution.py
@@ -291,7 +291,7 @@
     def send_steps(part, low, high):
         def one(step, carry):
             odd = lax.rem(step, 2)
-            offset = (2 * odd - 1) * (half - lax.div(step + odd, 2))
+            offset = (2 * odd - 1) * (1 - 2 * core) * (half - lax.div(step + odd, 2))
             z = z_off(offset)
             for k in range(2):
                 turn(part, 2 * z + k)
@@ -341,6 +341,7 @@
     ring_arrived(half)
     send_steps(1, 3, nz)
     forward(0)
+    forward(1)
 
     def leaf(slot, start, size):
         source = xor(i_at, slot, ibits)
@@ -376,10 +377,35 @@
 
     quarter = ni // 4
 
+    def arrived(part, n):
+        @pl.when(n == 0)
+        def _():
+            local_copy(part).wait()
+
+        @pl.when(n != 0)
+        def _():
+            block_arrival(part, n).wait_recv()
+
+        for m in (1, 2, 3):
+            slot = n + m * quarter
+            if m * quarter != 2 * half:
+                block_arrival(part, slot).wait_recv()
+                continue
+
+            @pl.when(n < 2)
+            def _():
+                for way in range(2):
+                    hop2_arrival(part, way, n).wait_recv()
+
+            @pl.when(n >= 2)
+            def _():
+                block_arrival(part, slot).wait_recv()
+
     def work(part):
         start, size, at, piece = parts[part]
 
         def group(n, carry):
+            arrived(part, n)
             kept, _ = leaf(n, start, size)
             given, limit = leaf(n + 2 * quarter, start, size)
             first_sum = kept + clipped(given, limit[0:1])
@@ -433,25 +459,18 @@
         out_ref[pl.ds(at, piece), :] = leaves[0][0:piece]
 
     for part in range(count):
-        local_copy(part).wait()
-        for slot in range(1, ni):
-            if slot // 2 == half:
-                for way in range(2):
-                    hop2_arrival(part, way, slot % 2).wait_recv()
-            else:
-                block_arrival(part, slot).wait_recv()
-        if part + 1 < count:
-            forward(part + 1)
-        if part + 2 < count:
-            send_steps(part + 2, 0, nz)
         if part == 0:
             for offset in range(nz):
                 twin(offset, 1 - core).wait_recv()
             for step in range(1, no):
                 limit_arrival(lax.rem(o_at + step, no)).wait_recv()
         work(part)
+        if part + 2 < count:
+            send_steps(part + 2, 0, nz)
         if part > 0:
             finish(part - 1)
+        if part + 2 < count:
+            forward(part + 2)
     finish(count - 1)
 
     for way in range(2):

time: 213 us -> 212 us (level)
  no operation moved by 1% of the time
where the time goes in v2:
time: 212 us
  Pallas kernels  211 us (100%)
    pallas_call x1, Pallas kernels, body(): pl.pallas_call(functools.partial(kernel, ni, no, parts, span), out_shape=...  211 us

profile of v2, /device:TPU:1, one launch (start us, length us, event | category | flops | bytes accessed | tf_op | source)
XLA Modules:
  0.0 212.1 jit_solution(3162778484720352404)
XLA Ops:
  0.0 210.5 %shard_map.37 = f32[58,512]{1,0:T(8,128)} custom-call(bf16[256,14848]{1,0:T(8,128)(2,1)} %acts_hbm.1, bf16[256,512]{1,0:T(8,128)(2,1)} %grad_hbm.1, s32[1,8]{1,0:T(1,128)} %shifts_smem.1), custom_call_target="tpu_custom_call" | custom-call | flops 3892314112 | bytes 7602176 | tf_op jit(solution)/shard_map/pallas_call | solution.py:518
  210.5 1.6 copy.5

commit v3 on v2

--- a/solution.py
+++ b/solution.py
@@ -329,19 +329,17 @@
         limit_copy(lax.rem(o_at + step, no)).start()
     for q in range(quarters):
         fetch(q).wait()
-    done = 0
-    for step in range(1, half):
-        upto = 2 * step + 1 if step < half - 1 else nz
-        send_steps(0, done, upto)
-        ring_arrived(step)
-        done = upto
-    if half == 1:
-        send_steps(0, 0, nz)
-    send_steps(1, 0, 3)
-    ring_arrived(half)
-    send_steps(1, 3, nz)
-    forward(0)
-    forward(1)
+    ahead = min(3, count)
+    turns = [(0, 0, 3), (0, 3, 5), (0, 5, nz), (1, 0, 3), (1, 3, nz)]
+    turns = [(part, low, min(high, nz)) for part, low, high in turns if low < nz and part < ahead]
+    turns += [(part, 0, nz) for part in range(2, ahead)]
+    waits = {0: 1, 1: 2, 3: 3, 4: 4}
+    for turn_at, (part, low, high) in enumerate(turns):
+        send_steps(part, low, high)
+        if waits.get(turn_at, half + 1) <= half:
+            ring_arrived(waits[turn_at])
+    for part in range(ahead):
+        forward(part)
 
     def leaf(slot, start, size):
         source = xor(i_at, slot, ibits)
@@ -458,27 +456,7 @@
             ]
         out_ref[pl.ds(at, piece), :] = leaves[0][0:piece]
 
-    for part in range(count):
-        if part == 0:
-            for offset in range(nz):
-                twin(offset, 1 - core).wait_recv()
-            for step in range(1, no):
-                limit_arrival(lax.rem(o_at + step, no)).wait_recv()
-        work(part)
-        if part + 2 < count:
-            send_steps(part + 2, 0, nz)
-        if part > 0:
-            finish(part - 1)
-        if part + 2 < count:
-            forward(part + 2)
-    finish(count - 1)
-
-    for way in range(2):
-        for step in range(1, half + 1):
-            ring(way, step).wait_send()
-    for offset in range(nz):
-        twin(offset, core).wait_send()
-    for part in range(count):
+    def sent(part):
         for slot in range(1, ni):
             if slot // 2 != half:
                 block_arrival(part, slot).wait_send()
@@ -488,8 +466,34 @@
                 hop2(part, way, k).wait_send()
         for step in range(1, no):
             out_copy(part, lax.rem(o_at + step, no)).wait_send()
-    for step in range(1, no):
-        limit_copy(lax.rem(o_at + step, no)).wait_send()
+
+    for part in range(count):
+        if part == 0:
+            for offset in range(nz):
+                twin(offset, 1 - core).wait_recv()
+            for step in range(1, no):
+                limit_arrival(lax.rem(o_at + step, no)).wait_recv()
+        if part + 1 == count:
+            for way in range(2):
+                for step in range(1, half + 1):
+                    ring(way, step).wait_send()
+            for offset in range(nz):
+                twin(offset, core).wait_send()
+            for step in range(1, no):
+                limit_copy(lax.rem(o_at + step, no)).wait_send()
+            for early in range(part):
+                sent(early)
+            if part > 0:
+                finish(part - 1)
+        work(part)
+        if part + ahead < count:
+            send_steps(part + ahead, 0, nz)
+        if 0 < part < count - 1:
+            finish(part - 1)
+        if part + ahead < count:
+            forward(part + ahead)
+    finish(count - 1)
+    sent(count - 1)
 
 
 def cut_parts(rows, no):

time: 212 us -> 210 us (level)
  Pallas kernels: 211 us -> 208 us
    pallas_call x1, Pallas kernels: 211 us -> 208 us  [body(): pl.pallas_call(functools.partial(kernel, ni, no, parts, span), out_shape=...]
where the time goes in v3:
time: 210 us
  Pallas kernels  208 us (99%)
    pallas_call x1, Pallas kernels, body(): pl.pallas_call(functools.partial(kernel, ni, no, parts, span), out_shape=...  208 us

profile of v3, /device:TPU:1, one launch (start us, length us, event | category | flops | bytes accessed | tf_op | source)
XLA Modules:
  0.0 209.9 jit_solution(2127069697886288383)
XLA Ops:
  0.0 208.3 %shard_map.37 = f32[58,512]{1,0:T(8,128)} custom-call(bf16[256,14848]{1,0:T(8,128)(2,1)} %acts_hbm.1, bf16[256,512]{1,0:T(8,128)(2,1)} %grad_hbm.1, s32[1,8]{1,0:T(1,128)} %shifts_smem.1), custom_call_target="tpu_custom_call" | custom-call | flops 3892314112 | bytes 7602176 | tf_op jit(solution)/shard_map/pallas_call | solution.py:522
  208.3 1.6 copy.5

commit v4 on v3

--- a/solution.py
+++ b/solution.py
@@ -38,13 +38,14 @@
     span,
     acts_hbm,
     grad_hbm,
-    shifts_smem,
+    shifts_hbm,
     out_ref,
     raw,
     acts_t,
     recv,
     relay,
     grads,
+    limits,
     sums,
     total,
     place,
@@ -53,12 +54,18 @@
     in_box,
     limit_box,
     limits_in,
+    shifts_smem,
+    shift_sem,
     fetch_sem,
     grad_sem,
     ring_send,
     ring_recv,
+    tile_send,
+    tile_recv,
     twin_send,
     twin_recv,
+    twin_tile_send,
+    twin_tile_recv,
     block_send,
     block_recv,
     hop1_send,
@@ -99,6 +106,8 @@
         cols = pl.ds(q * strip, strip)
         return pltpu.make_async_copy(acts_hbm.at[:, cols], raw.at[:, cols], fetch_sem.at[q])
 
+    shift_copy = pltpu.make_async_copy(shifts_hbm, shifts_smem, shift_sem)
+    shift_copy.start()
     grad_copy = pltpu.make_async_copy(grad_hbm, grads.at[i_at, pl.ds(0, tokens)], grad_sem)
     grad_copy.start()
     for q in range(quarters):
@@ -114,12 +123,14 @@
             barrier, inc=1, device_id=(i_at, lax.rem(o_at + step, no)), device_id_type=MESH
         )
 
-    row_at = lax.broadcasted_iota(jnp.int32, (BOUND_ROWS, keys), 0)
-    left_shift = jnp.zeros((BOUND_ROWS, keys), jnp.int32)
+    row_at = lax.broadcasted_iota(jnp.int32, (BOUND_ROWS, 128), 0)
+    left_shift = jnp.zeros((BOUND_ROWS, 128), jnp.int32)
+    shift_copy.wait()
     for hop in range(ibits + obits):
         left_shift = jnp.where(row_at == hop, 12 - shifts_smem[0, hop], left_shift)
     own_limits = jnp.left_shift(jnp.ones_like(left_shift), left_shift).astype(jnp.float32) * 0.109375
     own_limits = own_limits.astype(jnp.bfloat16)
+    limits[i_at, :, :] = own_limits
     limit_box[...] = own_limits
 
     def fill_place(ref, piece):
@@ -136,51 +147,80 @@
         fill_place(place_last, parts[-1][3])
 
     grad_copy.wait()
-    grads[i_at, pl.ds(tokens, BOUND_ROWS), :] = own_limits
-
     pl.semaphore_wait(barrier, ni + no - 2)
 
-    grad_rows = grads.shape[1]
-    cut = round_up(grad_rows // 2, 16)
+    cut = tokens // 2
 
     def ring(way, step):
         sign = 1 if way == 0 else -1
         source = 2 * z_off(sign * (1 - step)) + core
+        target = at_inner(z_off(sign), core)
         if step < half:
-            piece_at = pl.ds(0, grad_rows)
+            piece = grads.at[source]
         else:
-            piece_at = pl.ds(0, cut) if way == 0 else pl.ds(cut, grad_rows - cut)
-        piece = grads.at[source, piece_at]
-        return pltpu.make_async_remote_copy(
-            src_ref=piece,
-            dst_ref=piece,
-            send_sem=ring_send.at[way, step - 1],
-            recv_sem=ring_recv.at[way, step - 1],
-            device_id=at_inner(z_off(sign), core),
-            device_id_type=MESH,
-        )
+            piece = grads.at[source, pl.ds(way * cut, cut)]
+        copies = [
+            pltpu.make_async_remote_copy(
+                src_ref=piece,
+                dst_ref=piece,
+                send_sem=ring_send.at[way, step - 1],
+                recv_sem=ring_recv.at[way, step - 1],
+                device_id=target,
+                device_id_type=MESH,
+            )
+        ]
+        if step < half or way == 0:
+            copies.append(
+                pltpu.make_async_remote_copy(
+                    src_ref=limits.at[source],
+                    dst_ref=limits.at[source],
+                    send_sem=tile_send.at[way, step - 1],
+                    recv_sem=tile_recv.at[way, step - 1],
+                    device_id=target,
+                    device_id_type=MESH,
+                )
+            )
+        return copies
 
     def twin(offset, side):
         source = 2 * z_off(offset) + side
-        return pltpu.make_async_remote_copy(
-            src_ref=grads.at[source],
-            dst_ref=grads.at[source],
-            send_sem=twin_send.at[offset % nz],
-            recv_sem=twin_recv.at[offset % nz],
-            device_id=at_inner(z_at, 1 - core),
-            device_id_type=MESH,
-        )
+        return [
+            pltpu.make_async_remote_copy(
+                src_ref=ref.at[source],
+                dst_ref=ref.at[source],
+                send_sem=send.at[offset % nz],
+                recv_sem=recv_at.at[offset % nz],
+                device_id=at_inner(z_at, 1 - core),
+                device_id_type=MESH,
+            )
+            for ref, send, recv_at in (
+                (grads, twin_send, twin_recv),
+                (limits, twin_tile_send, twin_tile_recv),
+            )
+        ]
+
+    def start_all(copies):
+        for copy in copies:
+            copy.start()
+
+    def wait_sent(copies):
+        for copy in copies:
+            copy.wait_send()
+
+    def wait_arrived(copies):
+        for copy in copies:
+            copy.wait_recv()
 
     def ring_arrived(step):
-        ring(0, step).wait_recv()
-        ring(1, step).wait_recv()
+        wait_arrived(ring(0, step))
+        wait_arrived(ring(1, step))
         if step < half:
-            ring(0, step + 1).start()
-            ring(1, step + 1).start()
-            twin(-step, core).start()
-            twin(step, core).start()
+            start_all(ring(0, step + 1))
+            start_all(ring(1, step + 1))
+            start_all(twin(-step, core))
+            start_all(twin(step, core))
         else:
-            twin(half, core).start()
+            start_all(twin(half, core))
 
     def limit_copy(target):
         return pltpu.make_async_remote_copy(
@@ -322,9 +362,9 @@
                 hop1(part, way, k).wait_recv()
                 hop2(part, way, k).start()
 
-    ring(0, 1).start()
-    ring(1, 1).start()
-    twin(0, core).start()
+    start_all(ring(0, 1))
+    start_all(ring(1, 1))
+    start_all(twin(0, core))
     for step in range(1, no):
         limit_copy(lax.rem(o_at + step, no)).start()
     for q in range(quarters):
@@ -341,15 +381,17 @@
     for part in range(ahead):
         forward(part)
 
+    def wide(tile):
+        return jnp.tile(tile.astype(jnp.float32), (1, keys // 128))
+
     def leaf(slot, start, size):
         source = xor(i_at, slot, ibits)
         value = jnp.dot(
             recv[slot, pl.ds(start, size), :],
-            grads[source, pl.ds(0, tokens), :],
+            grads[source],
             preferred_element_type=jnp.float32,
         )
-        limit = grads[source, pl.ds(tokens, BOUND_ROWS), :].astype(jnp.float32)
-        return value, limit
+        return value, wide(limits[source])
 
     def out_copy(part, target):
         piece_at = pl.ds(parts[part][2], 16)
@@ -420,7 +462,7 @@
             width_now //= 2
             for n in range(width_now):
                 source = xor(i_at, n + width_now, ibits)
-                limit = grads[source, pl.ds(tokens, BOUND_ROWS), :].astype(jnp.float32)
+                limit = wide(limits[source])
                 value = sums[n, pl.ds(0, size), :] + clipped(
                     sums[n + width_now, pl.ds(0, size), :], limit[level : level + 1]
                 )
@@ -441,22 +483,22 @@
         for step in range(1, no):
             out_arrival(part, lax.rem(o_at + step, no)).wait_recv()
         leaves = [out_box[o_at, pl.ds(at, 16), :].astype(jnp.float32)]
-        limits = [None]
+        caps = [None]
         for slot in range(1, no):
             source = xor(o_at, slot, obits)
             leaves.append(in_box[source, pl.ds(at, 16), :].astype(jnp.float32))
-            limits.append(limits_in[source].astype(jnp.float32))
+            caps.append(wide(limits_in[source]))
         many = no
         for hop in range(obits):
             many //= 2
             level = ibits + hop
             leaves = [
-                leaves[n] + clipped(leaves[n + many], limits[n + many][level : level + 1])
+                leaves[n] + clipped(leaves[n + many], caps[n + many][level : level + 1])
                 for n in range(many)
             ]
         out_ref[pl.ds(at, piece), :] = leaves[0][0:piece]
 
-    def sent(part):
+    def blocks_sent(part):
         for slot in range(1, ni):
             if slot // 2 != half:
                 block_arrival(part, slot).wait_send()
@@ -464,25 +506,28 @@
             for k in range(2):
                 hop1(part, way, k).wait_send()
                 hop2(part, way, k).wait_send()
+
+    def pieces_sent(part):
         for step in range(1, no):
             out_copy(part, lax.rem(o_at + step, no)).wait_send()
 
     for part in range(count):
         if part == 0:
             for offset in range(nz):
-                twin(offset, 1 - core).wait_recv()
+                wait_arrived(twin(offset, 1 - core))
             for step in range(1, no):
                 limit_arrival(lax.rem(o_at + step, no)).wait_recv()
         if part + 1 == count:
             for way in range(2):
                 for step in range(1, half + 1):
-                    ring(way, step).wait_send()
+                    wait_sent(ring(way, step))
             for offset in range(nz):
-                twin(offset, core).wait_send()
+                wait_sent(twin(offset, core))
             for step in range(1, no):
                 limit_copy(lax.rem(o_at + step, no)).wait_send()
             for early in range(part):
-                sent(early)
+                blocks_sent(early)
+                pieces_sent(early)
             if part > 0:
                 finish(part - 1)
         work(part)
@@ -492,8 +537,9 @@
             finish(part - 1)
         if part + ahead < count:
             forward(part + ahead)
+    blocks_sent(count - 1)
     finish(count - 1)
-    sent(count - 1)
+    pieces_sent(count - 1)
 
 
 def cut_parts(rows, no):
@@ -521,11 +567,11 @@
     dma = pltpu.SemaphoreType.DMA
     return pl.pallas_call(
         functools.partial(kernel, ni, no, parts, span),
-        out_shape=jax.ShapeDtypeStruct((rows, keys), jnp.float32),
+        out_shape=pltpu.VMEM((rows, keys), jnp.float32),
         in_specs=[
             pl.BlockSpec(memory_space=pl.ANY),
             pl.BlockSpec(memory_space=pl.ANY),
-            pl.BlockSpec(memory_space=pltpu.SMEM),
+            pl.BlockSpec(memory_space=pl.ANY),
         ],
         out_specs=pl.BlockSpec(memory_space=pltpu.VMEM),
         scratch_shapes=[
@@ -533,19 +579,26 @@
             pltpu.VMEM((width, tokens), jnp.bfloat16),
             pltpu.VMEM((ni, block, tokens), jnp.bfloat16),
             pltpu.VMEM((2, block, tokens), jnp.bfloat16),
-            pltpu.VMEM((ni, tokens + BOUND_ROWS, keys), jnp.bfloat16),
+            pltpu.VMEM((ni, tokens, keys), jnp.bfloat16),
+            pltpu.VMEM((ni, BOUND_ROWS, 128), jnp.bfloat16),
             pltpu.VMEM((ni // 4, widest, keys), jnp.float32),
             pltpu.VMEM((widest, keys), jnp.float32),
             pltpu.VMEM((widest, span), jnp.int32),
             pltpu.VMEM((parts[-1][1], span), jnp.int32),
             pltpu.VMEM((no, padded, keys), jnp.bfloat16),
             pltpu.VMEM((no, padded, keys), jnp.bfloat16),
-            pltpu.VMEM((BOUND_ROWS, keys), jnp.bfloat16),
-            pltpu.VMEM((no, BOUND_ROWS, keys), jnp.bfloat16),
+            pltpu.VMEM((BOUND_ROWS, 128), jnp.bfloat16),
+            pltpu.VMEM((no, BOUND_ROWS, 128), jnp.bfloat16),
+            pltpu.SMEM(shifts.shape, jnp.int32),
+            dma,
             dma((4,)),
             dma,
             dma((2, half)),
             dma((2, half)),
+            dma((2, half)),
+            dma((2, half)),
+            dma((nz,)),
+            dma((nz,)),
             dma((nz,)),
             dma((nz,)),
             dma((count, ni)),

time: 210 us -> 207 us (0.986)
  no operation moved by 1% of the time
where the time goes in v4:
time: 207 us
  Pallas kernels  206 us (100%)
    pallas_call x1, Pallas kernels, body(): pl.pallas_call(functools.partial(kernel, ni, no, parts, span), out_shape=...  206 us

profile of v4, /device:TPU:1, one launch (start us, length us, event | category | flops | bytes accessed | tf_op | source)
XLA Modules:
  0.0 206.9 jit_solution(6221090634284343605)
XLA Ops:
  0.0 206.3 %shard_map.37 = f32[58,512]{1,0:T(8,128)S(1)} custom-call(bf16[256,14848]{1,0:T(8,128)(2,1)} %acts_hbm.1, bf16[256,512]{1,0:T(8,128)(2,1)} %grad_hbm.1, s32[1,8]{1,0:T(1,128)} %shifts_hbm.1), custom_call_target="tpu_custom_call" | custom-call | flops 3892314112 | bytes 7602176 | tf_op jit(solution)/shard_map/pallas_call | solution.py:568
  206.3 0.7 copy.5

commit v5 on v4

--- a/solution.py
+++ b/solution.py
@@ -328,13 +328,25 @@
             local_sem.at[part],
         )
 
-    def send_steps(part, low, high):
+    def z_of_step(step):
+        odd = lax.rem(step, 2)
+        return z_off((2 * odd - 1) * (1 - 2 * core) * (half - lax.div(step + odd, 2)))
+
+    def turn_steps(part, low, high):
         def one(step, carry):
-            odd = lax.rem(step, 2)
-            offset = (2 * odd - 1) * (1 - 2 * core) * (half - lax.div(step + odd, 2))
-            z = z_off(offset)
+            z = z_of_step(step)
             for k in range(2):
                 turn(part, 2 * z + k)
+            return carry
+
+        lax.fori_loop(low, high, one, 0)
+
+    def send_steps(part, low, high, turning=False):
+        def one(step, carry):
+            z = z_of_step(step)
+            if turning:
+                for k in range(2):
+                    turn(part, 2 * z + k)
 
             @pl.when(step == 0)
             def _():
@@ -369,17 +381,23 @@
         limit_copy(lax.rem(o_at + step, no)).start()
     for q in range(quarters):
         fetch(q).wait()
-    ahead = min(3, count)
-    turns = [(0, 0, 3), (0, 3, 5), (0, 5, nz), (1, 0, 3), (1, 3, nz)]
-    turns = [(part, low, min(high, nz)) for part, low, high in turns if low < nz and part < ahead]
-    turns += [(part, 0, nz) for part in range(2, ahead)]
-    waits = {0: 1, 1: 2, 3: 3, 4: 4}
-    for turn_at, (part, low, high) in enumerate(turns):
-        send_steps(part, low, high)
-        if waits.get(turn_at, half + 1) <= half:
-            ring_arrived(waits[turn_at])
-    for part in range(ahead):
-        forward(part)
+    far = min(3, nz)
+    near = min(5, nz)
+    send_steps(0, 0, far, turning=True)
+    ring_arrived(1)
+    send_steps(0, far, near, turning=True)
+    if half > 1:
+        ring_arrived(2)
+    send_steps(0, near, nz, turning=True)
+    if count > 1:
+        send_steps(1, 0, far, turning=True)
+    for step in range(3, half + 1):
+        ring_arrived(step)
+    forward(0)
+    if count > 1:
+        turn_steps(1, far, nz)
+    for part in range(2, count):
+        turn_steps(part, 0, nz)
 
     def wide(tile):
         return jnp.tile(tile.astype(jnp.float32), (1, keys // 128))
@@ -445,7 +463,8 @@
         start, size, at, piece = parts[part]
 
         def group(n, carry):
-            arrived(part, n)
+            if part + 1 == count:
+                arrived(part, n)
             kept, _ = leaf(n, start, size)
             given, limit = leaf(n + 2 * quarter, start, size)
             first_sum = kept + clipped(given, limit[0:1])
@@ -512,11 +531,6 @@
             out_copy(part, lax.rem(o_at + step, no)).wait_send()
 
     for part in range(count):
-        if part == 0:
-            for offset in range(nz):
-                wait_arrived(twin(offset, 1 - core))
-            for step in range(1, no):
-                limit_arrival(lax.rem(o_at + step, no)).wait_recv()
         if part + 1 == count:
             for way in range(2):
                 for step in range(1, half + 1):
@@ -530,13 +544,21 @@
                 pieces_sent(early)
             if part > 0:
                 finish(part - 1)
+        else:
+            for n in range(quarter):
+                arrived(part, jnp.int32(n))
+            forward(part + 1)
+            send_steps(part + 1, far, nz)
+            if part + 2 < count:
+                send_steps(part + 2, 0, far)
+        if part == 0:
+            for offset in range(nz):
+                wait_arrived(twin(offset, 1 - core))
+            for step in range(1, no):
+                limit_arrival(lax.rem(o_at + step, no)).wait_recv()
         work(part)
-        if part + ahead < count:
-            send_steps(part + ahead, 0, nz)
         if 0 < part < count - 1:
             finish(part - 1)
-        if part + ahead < count:
-            forward(part + ahead)
     blocks_sent(count - 1)
     finish(count - 1)
     pieces_sent(count - 1)

time: 207 us -> 213 us (1.029)
  Pallas kernels: 206 us -> 212 us
    pallas_call x1, Pallas kernels: 206 us -> 212 us  [body(): pl.pallas_call(functools.partial(kernel, ni, no, parts, span), out_shape=...]
where the time goes in v5:
time: 213 us
  Pallas kernels  212 us (100%)
    pallas_call x1, Pallas kernels, body(): pl.pallas_call(functools.partial(kernel, ni, no, parts, span), out_shape=...  212 us

profile of v5, /device:TPU:1, one launch (start us, length us, event | category | flops | bytes accessed | tf_op | source)
XLA Modules:
  0.0 212.9 jit_solution(7602912716962105428)
XLA Ops:
  0.0 212.2 %shard_map.37 = f32[58,512]{1,0:T(8,128)S(1)} custom-call(bf16[256,14848]{1,0:T(8,128)(2,1)} %acts_hbm.1, bf16[256,512]{1,0:T(8,128)(2,1)} %grad_hbm.1, s32[1,8]{1,0:T(1,128)} %shifts_hbm.1), custom_call_target="tpu_custom_call" | custom-call | flops 3892314112 | bytes 7602176 | tf_op jit(solution)/shard_map/pallas_call | solution.py:590
  212.2 0.7 copy.5

commit v6 on v4

--- a/solution.py
+++ b/solution.py
@@ -369,7 +369,7 @@
         limit_copy(lax.rem(o_at + step, no)).start()
     for q in range(quarters):
         fetch(q).wait()
-    ahead = min(3, count)
+    ahead = count
     turns = [(0, 0, 3), (0, 3, 5), (0, 5, nz), (1, 0, 3), (1, 3, nz)]
     turns = [(part, low, min(high, nz)) for part, low, high in turns if low < nz and part < ahead]
     turns += [(part, 0, nz) for part in range(2, ahead)]

time: 207 us -> 214 us (1.034)
  Pallas kernels: 206 us -> 213 us
    pallas_call x1, Pallas kernels: 206 us -> 213 us  [body(): pl.pallas_call(functools.partial(kernel, ni, no, parts, span), out_shape=...]
where the time goes in v6:
time: 214 us
  Pallas kernels  213 us (100%)
    pallas_call x1, Pallas kernels, body(): pl.pallas_call(functools.partial(kernel, ni, no, parts, span), out_shape=...  213 us

profile of v6, /device:TPU:1, one launch (start us, length us, event | category | flops | bytes accessed | tf_op | source)
XLA Modules:
  0.0 213.9 jit_solution(1121031319618576953)
XLA Ops:
  0.0 213.2 %shard_map.37 = f32[58,512]{1,0:T(8,128)S(1)} custom-call(bf16[256,14848]{1,0:T(8,128)(2,1)} %acts_hbm.1, bf16[256,512]{1,0:T(8,128)(2,1)} %grad_hbm.1, s32[1,8]{1,0:T(1,128)} %shifts_hbm.1), custom_call_target="tpu_custom_call" | custom-call | flops 3892314112 | bytes 7602176 | tf_op jit(solution)/shard_map/pallas_call | solution.py:568
  213.2 0.7 copy.5

commit v7 on v5

--- a/solution.py
+++ b/solution.py
@@ -332,6 +332,30 @@
         odd = lax.rem(step, 2)
         return z_off((2 * odd - 1) * (1 - 2 * core) * (half - lax.div(step + odd, 2)))
 
+    def by_step(part, step, act):
+        z = z_of_step(step)
+
+        @pl.when(step == 0)
+        def _():
+            for way in range(2):
+                for k in range(2):
+                    act(hop1(part, way, k))
+
+        @pl.when(jnp.logical_and(step > 0, step < nz - 1))
+        def _():
+            for k in range(2):
+                act(block_copy(part, 2 * z + k))
+
+        @pl.when(step == nz - 1)
+        def _():
+            act(block_copy(part, 2 * z_at + 1 - core))
+
+    def start(copy):
+        copy.start()
+
+    def leave(copy):
+        copy.wait_send()
+
     def turn_steps(part, low, high):
         def one(step, carry):
             z = z_of_step(step)
@@ -340,30 +364,32 @@
             return carry
 
         lax.fori_loop(low, high, one, 0)
-
-    def send_steps(part, low, high, turning=False):
+        if high == nz:
+            local_copy(part).start()
+
+    def first_steps(part, low, high):
         def one(step, carry):
             z = z_of_step(step)
-            if turning:
-                for k in range(2):
-                    turn(part, 2 * z + k)
-
-            @pl.when(step == 0)
-            def _():
-                for way in range(2):
-                    for k in range(2):
-                        hop1(part, way, k).start()
-
-            @pl.when(jnp.logical_and(step > 0, step < nz - 1))
-            def _():
-                for k in range(2):
-                    block_copy(part, 2 * z + k).start()
-
-            @pl.when(step == nz - 1)
-            def _():
-                block_copy(part, 2 * z_at + 1 - core).start()
-                local_copy(part).start()
-
+            for k in range(2):
+                turn(part, 2 * z + k)
+            by_step(part, step, start)
+            return carry
+
+        lax.fori_loop(low, high, one, 0)
+        if high == nz:
+            local_copy(part).start()
+
+    def wait_steps(part, low, high):
+        def one(step, carry):
+            by_step(part, step, leave)
+            return carry
+
+        lax.fori_loop(low, high, one, 0)
+
+    def next_steps(part, low, high, part_before, low_before):
+        def one(step, carry):
+            by_step(part_before, step - low + low_before, leave)
+            by_step(part, step, start)
             return carry
 
         lax.fori_loop(low, high, one, 0)
@@ -383,21 +409,21 @@
         fetch(q).wait()
     far = min(3, nz)
     near = min(5, nz)
-    send_steps(0, 0, far, turning=True)
+    first_steps(0, 0, far)
     ring_arrived(1)
-    send_steps(0, far, near, turning=True)
+    first_steps(0, far, near)
     if half > 1:
         ring_arrived(2)
-    send_steps(0, near, nz, turning=True)
+    first_steps(0, near, nz)
     if count > 1:
-        send_steps(1, 0, far, turning=True)
+        first_steps(1, 0, far)
     for step in range(3, half + 1):
         ring_arrived(step)
     forward(0)
     if count > 1:
         turn_steps(1, far, nz)
-    for part in range(2, count):
-        turn_steps(part, 0, nz)
+    if count > 2:
+        turn_steps(2, 0, nz)
 
     def wide(tile):
         return jnp.tile(tile.astype(jnp.float32), (1, keys // 128))
@@ -463,8 +489,7 @@
         start, size, at, piece = parts[part]
 
         def group(n, carry):
-            if part + 1 == count:
-                arrived(part, n)
+            arrived(part, n)
             kept, _ = leaf(n, start, size)
             given, limit = leaf(n + 2 * quarter, start, size)
             first_sum = kept + clipped(given, limit[0:1])
@@ -517,20 +542,26 @@
             ]
         out_ref[pl.ds(at, piece), :] = leaves[0][0:piece]
 
-    def blocks_sent(part):
-        for slot in range(1, ni):
-            if slot // 2 != half:
-                block_arrival(part, slot).wait_send()
-        for way in range(2):
-            for k in range(2):
-                hop1(part, way, k).wait_send()
-                hop2(part, way, k).wait_send()
-
     def pieces_sent(part):
         for step in range(1, no):
             out_copy(part, lax.rem(o_at + step, no)).wait_send()
 
+    def relays_sent(part):
+        for way in range(2):
+            for k in range(2):
+                hop2(part, way, k).wait_send()
+
     for part in range(count):
+        if part + 1 < count:
+            next_steps(part + 1, far, nz, part, 0)
+            forward(part + 1)
+        if part + 2 < count:
+            next_steps(part + 2, 0, far, part, nz - far)
+        if part == 0:
+            for offset in range(nz):
+                wait_arrived(twin(offset, 1 - core))
+            for step in range(1, no):
+                limit_arrival(lax.rem(o_at + step, no)).wait_recv()
         if part + 1 == count:
             for way in range(2):
                 for step in range(1, half + 1):
@@ -539,27 +570,20 @@
                 wait_sent(twin(offset, core))
             for step in range(1, no):
                 limit_copy(lax.rem(o_at + step, no)).wait_send()
+            if part > 0:
+                wait_steps(part - 1, nz - far, nz)
             for early in range(part):
-                blocks_sent(early)
+                relays_sent(early)
                 pieces_sent(early)
             if part > 0:
                 finish(part - 1)
-        else:
-            for n in range(quarter):
-                arrived(part, jnp.int32(n))
-            forward(part + 1)
-            send_steps(part + 1, far, nz)
-            if part + 2 < count:
-                send_steps(part + 2, 0, far)
-        if part == 0:
-            for offset in range(nz):
-                wait_arrived(twin(offset, 1 - core))
-            for step in range(1, no):
-                limit_arrival(lax.rem(o_at + step, no)).wait_recv()
         work(part)
         if 0 < part < count - 1:
             finish(part - 1)
-    blocks_sent(count - 1)
+        if part + 3 < count:
+            turn_steps(part + 3, 0, nz)
+    wait_steps(count - 1, 0, nz)
+    relays_sent(count - 1)
     finish(count - 1)
     pieces_sent(count - 1)
 

time: 213 us -> 210 us (0.986)
  Pallas kernels: 212 us -> 209 us
    pallas_call x1, Pallas kernels: 212 us -> 209 us  [body(): pl.pallas_call(functools.partial(kernel, ni, no, parts, span), out_shape=...]
where the time goes in v7:
time: 210 us
  Pallas kernels  209 us (100%)
    pallas_call x1, Pallas kernels, body(): pl.pallas_call(functools.partial(kernel, ni, no, parts, span), out_shape=...  209 us

profile of v7, /device:TPU:1, one launch (start us, length us, event | category | flops | bytes accessed | tf_op | source)
XLA Modules:
  0.0 209.9 jit_solution(18075057795645306567)
XLA Ops:
  0.0 209.2 %shard_map.37 = f32[58,512]{1,0:T(8,128)S(1)} custom-call(bf16[256,14848]{1,0:T(8,128)(2,1)} %acts_hbm.1, bf16[256,512]{1,0:T(8,128)(2,1)} %grad_hbm.1, s32[1,8]{1,0:T(1,128)} %shifts_hbm.1), custom_call_target="tpu_custom_call" | custom-call | flops 3892314112 | bytes 7602176 | tf_op jit(solution)/shard_map/pallas_call | solution.py:614
  209.3 0.7 copy.5

commit v8 on v7

--- a/solution.py
+++ b/solution.py
@@ -20,6 +20,10 @@
 
 
 def clipped(values, bound):
+    return jnp.clip(values, -bound, bound)
+
+
+def rounded(values, bound):
     return jnp.clip(values, -bound, bound).astype(jnp.bfloat16).astype(jnp.float32)
 
 
@@ -417,13 +421,21 @@
     first_steps(0, near, nz)
     if count > 1:
         first_steps(1, 0, far)
-    for step in range(3, half + 1):
+    if half > 2:
+        ring_arrived(3)
+    if count > 1:
+        first_steps(1, far, nz)
+    for step in range(4, half + 1):
         ring_arrived(step)
     forward(0)
+    if count > 2:
+        first_steps(2, 0, far)
     if count > 1:
-        turn_steps(1, far, nz)
+        forward(1)
     if count > 2:
-        turn_steps(2, 0, nz)
+        turn_steps(2, far, nz)
+    for part in range(3, count):
+        turn_steps(part, 0, nz)
 
     def wide(tile):
         return jnp.tile(tile.astype(jnp.float32), (1, keys // 128))
@@ -537,7 +549,7 @@
             many //= 2
             level = ibits + hop
             leaves = [
-                leaves[n] + clipped(leaves[n + many], caps[n + many][level : level + 1])
+                leaves[n] + rounded(leaves[n + many], caps[n + many][level : level + 1])
                 for n in range(many)
             ]
         out_ref[pl.ds(at, piece), :] = leaves[0][0:piece]
@@ -552,11 +564,11 @@
                 hop2(part, way, k).wait_send()
 
     for part in range(count):
-        if part + 1 < count:
-            next_steps(part + 1, far, nz, part, 0)
-            forward(part + 1)
         if part + 2 < count:
-            next_steps(part + 2, 0, far, part, nz - far)
+            next_steps(part + 2, far, nz, part, 0)
+            forward(part + 2)
+        if part + 3 < count:
+            next_steps(part + 3, 0, far, part, nz - far)
         if part == 0:
             for offset in range(nz):
                 wait_arrived(twin(offset, 1 - core))
@@ -570,8 +582,10 @@
                 wait_sent(twin(offset, core))
             for step in range(1, no):
                 limit_copy(lax.rem(o_at + step, no)).wait_send()
+            if part > 1:
+                wait_steps(part - 2, nz - far, nz)
             if part > 0:
-                wait_steps(part - 1, nz - far, nz)
+                wait_steps(part - 1, 0, nz)
             for early in range(part):
                 relays_sent(early)
                 pieces_sent(early)
@@ -580,8 +594,6 @@
         work(part)
         if 0 < part < count - 1:
             finish(part - 1)
-        if part + 3 < count:
-            turn_steps(part + 3, 0, nz)
     wait_steps(count - 1, 0, nz)
     relays_sent(count - 1)
     finish(count - 1)

time: 210 us -> 207 us (0.986)
  Pallas kernels: 209 us -> 206 us
    pallas_call x1, Pallas kernels: 209 us -> 206 us  [body(): pl.pallas_call(functools.partial(kernel, ni, no, parts, span), out_shape=...]
where the time goes in v8:
time: 207 us
  Pallas kernels  206 us (100%)
    pallas_call x1, Pallas kernels, body(): pl.pallas_call(functools.partial(kernel, ni, no, parts, span), out_shape=...  206 us

profile of v8, /device:TPU:1, one launch (start us, length us, event | category | flops | bytes accessed | tf_op | source)
XLA Modules:
  0.0 206.5 jit_solution(14257258974640059676)
XLA Ops:
  0.0 205.9 %shard_map.37 = f32[58,512]{1,0:T(8,128)S(1)} custom-call(bf16[256,14848]{1,0:T(8,128)(2,1)} %acts_hbm.1, bf16[256,512]{1,0:T(8,128)(2,1)} %grad_hbm.1, s32[1,8]{1,0:T(1,128)} %shifts_hbm.1), custom_call_target="tpu_custom_call" | custom-call | flops 3892314112 | bytes 7602176 | tf_op jit(solution)/shard_map/pallas_call | solution.py:626
  205.9 0.7 copy.5

commit v9 on v8

--- a/solution.py
+++ b/solution.py
@@ -20,10 +20,6 @@
 
 
 def clipped(values, bound):
-    return jnp.clip(values, -bound, bound)
-
-
-def rounded(values, bound):
     return jnp.clip(values, -bound, bound).astype(jnp.bfloat16).astype(jnp.float32)
 
 
@@ -159,20 +155,20 @@
         sign = 1 if way == 0 else -1
         source = 2 * z_off(sign * (1 - step)) + core
         target = at_inner(z_off(sign), core)
-        if step < half:
-            piece = grads.at[source]
-        else:
-            piece = grads.at[source, pl.ds(way * cut, cut)]
-        copies = [
-            pltpu.make_async_remote_copy(
-                src_ref=piece,
-                dst_ref=piece,
-                send_sem=ring_send.at[way, step - 1],
-                recv_sem=ring_recv.at[way, step - 1],
-                device_id=target,
-                device_id_type=MESH,
+        pieces = (0, 1) if step < half else (way,)
+        copies = []
+        for n in pieces:
+            piece = grads.at[source, pl.ds(n * cut, cut)]
+            copies.append(
+                pltpu.make_async_remote_copy(
+                    src_ref=piece,
+                    dst_ref=piece,
+                    send_sem=ring_send.at[way, step - 1, n],
+                    recv_sem=ring_recv.at[way, step - 1, n],
+                    device_id=target,
+                    device_id_type=MESH,
+                )
             )
-        ]
         if step < half or way == 0:
             copies.append(
                 pltpu.make_async_remote_copy(
@@ -412,26 +408,23 @@
     for q in range(quarters):
         fetch(q).wait()
     far = min(3, nz)
-    near = min(5, nz)
-    first_steps(0, 0, far)
+    first_steps(0, 0, nz)
     ring_arrived(1)
-    first_steps(0, far, near)
+    forward(0)
+    if count > 1:
+        first_steps(1, 0, far)
     if half > 1:
         ring_arrived(2)
-    first_steps(0, near, nz)
     if count > 1:
-        first_steps(1, 0, far)
+        first_steps(1, far, nz)
     if half > 2:
         ring_arrived(3)
     if count > 1:
-        first_steps(1, far, nz)
+        forward(1)
+    if count > 2:
+        first_steps(2, 0, far)
     for step in range(4, half + 1):
         ring_arrived(step)
-    forward(0)
-    if count > 2:
-        first_steps(2, 0, far)
-    if count > 1:
-        forward(1)
     if count > 2:
         turn_steps(2, far, nz)
     for part in range(3, count):
@@ -549,7 +542,7 @@
             many //= 2
             level = ibits + hop
             leaves = [
-                leaves[n] + rounded(leaves[n + many], caps[n + many][level : level + 1])
+                leaves[n] + clipped(leaves[n + many], caps[n + many][level : level + 1])
                 for n in range(many)
             ]
         out_ref[pl.ds(at, piece), :] = leaves[0][0:piece]
@@ -651,8 +644,8 @@
             dma,
             dma((4,)),
             dma,
-            dma((2, half)),
-            dma((2, half)),
+            dma((2, half, 2)),
+            dma((2, half, 2)),
             dma((2, half)),
             dma((2, half)),
             dma((nz,)),

time: 207 us -> 207 us (level)
  no operation moved by 1% of the time
where the time goes in v9:
time: 207 us
  Pallas kernels  206 us (100%)
    pallas_call x1, Pallas kernels, body(): pl.pallas_call(functools.partial(kernel, ni, no, parts, span), out_shape=...  206 us

profile of v9, /device:TPU:1, one launch (start us, length us, event | category | flops | bytes accessed | tf_op | source)
XLA Modules:
  0.0 206.8 jit_solution(3445088781570424719)
XLA Ops:
  0.0 206.2 %shard_map.37 = f32[58,512]{1,0:T(8,128)S(1)} custom-call(bf16[256,14848]{1,0:T(8,128)(2,1)} %acts_hbm.1, bf16[256,512]{1,0:T(8,128)(2,1)} %grad_hbm.1, s32[1,8]{1,0:T(1,128)} %shifts_hbm.1), custom_call_target="tpu_custom_call" | custom-call | flops 3892314112 | bytes 7602176 | tf_op jit(solution)/shard_map/pallas_call | solution.py:619
  206.2 0.7 copy.5

commit v10 on v9

--- a/solution.py
+++ b/solution.py
@@ -493,7 +493,8 @@
     def work(part):
         start, size, at, piece = parts[part]
 
-        def group(n, carry):
+        def group(index, carry):
+            n = quarter - 1 - index
             arrived(part, n)
             kept, _ = leaf(n, start, size)
             given, limit = leaf(n + 2 * quarter, start, size)
@@ -558,8 +559,8 @@
 
     for part in range(count):
         if part + 2 < count:
+            forward(part + 2)
             next_steps(part + 2, far, nz, part, 0)
-            forward(part + 2)
         if part + 3 < count:
             next_steps(part + 3, 0, far, part, nz - far)
         if part == 0:

time: 207 us -> 208 us (level)
  no operation moved by 1% of the time
where the time goes in v10:
time: 208 us
  Pallas kernels  207 us (100%)
    pallas_call x1, Pallas kernels, body(): pl.pallas_call(functools.partial(kernel, ni, no, parts, span), out_shape=...  207 us

profile of v10, /device:TPU:1, one launch (start us, length us, event | category | flops | bytes accessed | tf_op | source)
XLA Modules:
  0.0 207.7 jit_solution(9902601301976673790)
XLA Ops:
  0.0 207.0 %shard_map.37 = f32[58,512]{1,0:T(8,128)S(1)} custom-call(bf16[256,14848]{1,0:T(8,128)(2,1)} %acts_hbm.1, bf16[256,512]{1,0:T(8,128)(2,1)} %grad_hbm.1, s32[1,8]{1,0:T(1,128)} %shifts_hbm.1), custom_call_target="tpu_custom_call" | custom-call | flops 3892314112 | bytes 7602176 | tf_op jit(solution)/shard_map/pallas_call | solution.py:620
  207.0 0.7 copy.5

commit v11 on v10

--- a/solution.py
+++ b/solution.py
@@ -48,8 +48,7 @@
     limits,
     sums,
     total,
-    place,
-    place_last,
+    places,
     out_box,
     in_box,
     limit_box,
@@ -142,9 +141,9 @@
         for n in range(span // 128):
             ref[:, pl.ds(n * 128, 128)] = offset + n * 128
 
-    fill_place(place, parts[0][3])
-    if place_last is not None:
-        fill_place(place_last, parts[-1][3])
+    kinds = sorted(set(piece for _, _, _, piece in parts))
+    for kind, ref in zip(kinds, places):
+        fill_place(ref, kind)
 
     grad_copy.wait()
     pl.semaphore_wait(barrier, ni + no - 2)
@@ -246,7 +245,7 @@
         start, size, at, piece = parts[part]
         column = target * block
         tile = lax.div(column, 128)
-        source = place if piece == parts[0][3] else place_last
+        source = places[kinds.index(piece)]
         pick = (source[...] == column - tile * 128 + at).astype(jnp.bfloat16)
         window = raw[:, pl.ds(pl.multiple_of(tile * 128, 128), span)]
         acts_t[pl.ds(aligned(column + start), size), :] = lax.dot_general(
@@ -443,7 +442,7 @@
         return value, wide(limits[source])
 
     def out_copy(part, target):
-        piece_at = pl.ds(parts[part][2], 16)
+        piece_at = pl.ds(parts[part][2], round_up(parts[part][3], 16))
         return pltpu.make_async_remote_copy(
             src_ref=out_box.at[target, piece_at],
             dst_ref=in_box.at[o_at, piece_at],
@@ -454,7 +453,7 @@
         )
 
     def out_arrival(part, source):
-        piece_at = pl.ds(parts[part][2], 16)
+        piece_at = pl.ds(parts[part][2], round_up(parts[part][3], 16))
         return pltpu.make_async_remote_copy(
             src_ref=in_box.at[source, piece_at],
             dst_ref=in_box.at[source, piece_at],
@@ -492,6 +491,7 @@
 
     def work(part):
         start, size, at, piece = parts[part]
+        high = round_up(piece, 16)
 
         def group(index, carry):
             n = quarter - 1 - index
@@ -522,7 +522,7 @@
                     sums[n, pl.ds(0, size), :] = value
             level += 1
         for owner in range(no):
-            out_box[owner, pl.ds(at, 16), :] = total[pl.ds(owner * piece, 16), :].astype(
+            out_box[owner, pl.ds(at, high), :] = total[pl.ds(owner * piece, high), :].astype(
                 jnp.bfloat16
             )
         for step in range(1, no):
@@ -530,13 +530,14 @@
 
     def finish(part):
         _, _, at, piece = parts[part]
+        high = round_up(piece, 16)
         for step in range(1, no):
             out_arrival(part, lax.rem(o_at + step, no)).wait_recv()
-        leaves = [out_box[o_at, pl.ds(at, 16), :].astype(jnp.float32)]
+        leaves = [out_box[o_at, pl.ds(at, high), :].astype(jnp.float32)]
         caps = [None]
         for slot in range(1, no):
             source = xor(o_at, slot, obits)
-            leaves.append(in_box[source, pl.ds(at, 16), :].astype(jnp.float32))
+            leaves.append(in_box[source, pl.ds(at, high), :].astype(jnp.float32))
             caps.append(wide(limits_in[source]))
         many = no
         for hop in range(obits):
@@ -595,9 +596,13 @@
 
 
 def cut_parts(rows, no):
-    return tuple(
-        (no * at, no * min(16, rows - at), at, min(16, rows - at)) for at in range(0, rows, 16)
-    )
+    parts, at = [], 0
+    for piece in (16, 32, 16, 16):
+        piece = min(piece, rows - at)
+        if piece > 0:
+            parts.append((no * at, no * piece, at, piece))
+        at += piece
+    return tuple(parts)
 
 
 def body(acts, key_grad, shifts):
@@ -611,7 +616,8 @@
     half = nz // 2
     parts = cut_parts(rows, no)
     count = len(parts)
-    widest = parts[0][1]
+    widest = max(size for _, size, _, _ in parts)
+    kinds = sorted(set((piece, size) for _, size, _, piece in parts))
     span = max(
         round_up(block * (n + 1), 128) - block * n // 128 * 128 for n in range(ni)
     )
@@ -634,9 +640,8 @@
             pltpu.VMEM((ni, tokens, keys), jnp.bfloat16),
             pltpu.VMEM((ni, BOUND_ROWS, 128), jnp.bfloat16),
             pltpu.VMEM((ni // 4, widest, keys), jnp.float32),
-            pltpu.VMEM((widest, keys), jnp.float32),
-            pltpu.VMEM((widest, span), jnp.int32),
-            pltpu.VMEM((parts[-1][1], span), jnp.int32),
+            pltpu.VMEM((round_up(widest + 16, 16), keys), jnp.float32),
+            [pltpu.VMEM((size, span), jnp.int32) for _, size in kinds],
             pltpu.VMEM((no, padded, keys), jnp.bfloat16),
             pltpu.VMEM((no, padded, keys), jnp.bfloat16),
             pltpu.VMEM((BOUND_ROWS, 128), jnp.bfloat16),

time: 208 us -> 207 us (level)
  no operation moved by 1% of the time
where the time goes in v11:
time: 207 us
  Pallas kernels  206 us (100%)
    pallas_call x1, Pallas kernels, body(): pl.pallas_call(functools.partial(kernel, ni, no, parts, span), out_shape=...  206 us

profile of v11, /device:TPU:1, one launch (start us, length us, event | category | flops | bytes accessed | tf_op | source)
XLA Modules:
  0.0 207.0 jit_solution(16288660914218377953)
XLA Ops:
  0.0 206.3 %shard_map.37 = f32[58,512]{1,0:T(8,128)S(1)} custom-call(bf16[256,14848]{1,0:T(8,128)(2,1)} %acts_hbm.1, bf16[256,512]{1,0:T(8,128)(2,1)} %grad_hbm.1, s32[1,8]{1,0:T(1,128)} %shifts_hbm.1), custom_call_target="tpu_custom_call" | custom-call | flops 3892314112 | bytes 7602176 | tf_op jit(solution)/shard_map/pallas_call | solution.py:626
  206.3 0.7 copy.5

commit v12 on v11

--- a/solution.py
+++ b/solution.py
@@ -109,9 +109,6 @@
     shift_copy.start()
     grad_copy = pltpu.make_async_copy(grad_hbm, grads.at[i_at, pl.ds(0, tokens)], grad_sem)
     grad_copy.start()
-    for q in range(quarters):
-        fetch(q).start()
-
     barrier = pltpu.get_barrier_semaphore()
     for step in range(1, ni):
         pl.semaphore_signal(
@@ -121,6 +118,9 @@
         pl.semaphore_signal(
             barrier, inc=1, device_id=(i_at, lax.rem(o_at + step, no)), device_id_type=MESH
         )
+
+    for q in range(quarters):
+        fetch(q).start()
 
     row_at = lax.broadcasted_iota(jnp.int32, (BOUND_ROWS, 128), 0)
     left_shift = jnp.zeros((BOUND_ROWS, 128), jnp.int32)
@@ -142,8 +142,6 @@
             ref[:, pl.ds(n * 128, 128)] = offset + n * 128
 
     kinds = sorted(set(piece for _, _, _, piece in parts))
-    for kind, ref in zip(kinds, places):
-        fill_place(ref, kind)
 
     grad_copy.wait()
     pl.semaphore_wait(barrier, ni + no - 2)
@@ -402,12 +400,17 @@
     start_all(ring(0, 1))
     start_all(ring(1, 1))
     start_all(twin(0, core))
+    first_kind = kinds.index(parts[0][3])
+    fill_place(places[first_kind], kinds[first_kind])
     for step in range(1, no):
         limit_copy(lax.rem(o_at + step, no)).start()
     for q in range(quarters):
         fetch(q).wait()
     far = min(3, nz)
     first_steps(0, 0, nz)
+    for n, kind in enumerate(kinds):
+        if n != first_kind:
+            fill_place(places[n], kind)
     ring_arrived(1)
     forward(0)
     if count > 1:

time: 207 us -> 206 us (level)
  no operation moved by 1% of the time
where the time goes in v12:
time: 206 us
  Pallas kernels  206 us (100%)
    pallas_call x1, Pallas kernels, body(): pl.pallas_call(functools.partial(kernel, ni, no, parts, span), out_shape=...  206 us

profile of v12, /device:TPU:1, one launch (start us, length us, event | category | flops | bytes accessed | tf_op | source)
XLA Modules:
  0.0 206.4 jit_solution(13389076686651933236)
XLA Ops:
  0.0 205.7 %shard_map.37 = f32[58,512]{1,0:T(8,128)S(1)} custom-call(bf16[256,14848]{1,0:T(8,128)(2,1)} %acts_hbm.1, bf16[256,512]{1,0:T(8,128)(2,1)} %grad_hbm.1, s32[1,8]{1,0:T(1,128)} %shifts_hbm.1), custom_call_target="tpu_custom_call" | custom-call | flops 3892314112 | bytes 7602176 | tf_op jit(solution)/shard_map/pallas_call | solution.py:629
  205.7 0.7 copy.5
